TPU v7x, 32 devices: a whole 2x2x4 slice. The times are simulated.
32 devices in a mesh: dap: 16 (over z, y, core), heads: 2 (over x).
Axes of the slice: x: 2, y: 2, z: 4, core: 2. Of those that a mesh axis runs over, the one named last changes fastest.
Arguments:
- pair: bfloat16 [96, 96, 128], P('dap'), may hold values from -6 to 6
- ln_gain: float32 [128], replicated, may hold values from 0.1 to 1.9
- ln_shift: float32 [128], replicated, may hold values from -3 to 3
- w_project: bfloat16 [128, 4, 128], P(None, None, 'heads'), may hold values from -0.5 to 0.5
- w_bias: bfloat16 [128, 4], P(None, 'heads'), may hold values from -2 to 2
- w_out: bfloat16 [128, 128], P('heads'), may hold values from -0.5 to 0.5
Outputs:
- update: bfloat16 [96, 96, 128], P(('dap', 'heads'))
All inputs are finite; a program needn't handle non-finite values.
Results may differ from a plain program's by a relative error of at most 0.0039.
The roundings to bfloat16 on the way count: a program that leaves them out, or rounds other values in their place, can miss the bound.
Values may be sent and summed in bfloat16 or wider, within the bound.
A program may use at most 64 MiB of HBM per device.

v0:
```python
import math

import jax
import jax.numpy as jnp
from jax import lax
from jax.sharding import PartitionSpec as P


def normalize(pair, ln_gain, ln_shift):
    values_f = pair.astype(jnp.float32)
    average = jnp.mean(values_f, axis=-1, keepdims=True)
    centred = values_f - average
    variance = jnp.mean(centred * centred, axis=-1, keepdims=True)
    return (centred * lax.rsqrt(variance + 1e-05) * ln_gain + ln_shift).astype(jnp.bfloat16)


def project_entries(normed, flat_w):
    projected = jnp.dot(normed, flat_w, preferred_element_type=jnp.float32)
    head_width = flat_w.shape[1] // 4
    head_part = projected[..., : 3 * head_width].astype(jnp.bfloat16)
    gating = jax.nn.sigmoid(projected[..., 3 * head_width :]).astype(jnp.bfloat16)
    return jnp.concatenate([head_part, gating], axis=-1)


def local(pair, ln_gain, ln_shift, w_project, w_bias, w_out):
    row_count, width_n, channels = pair.shape
    heads_here = w_bias.shape[1]
    head_size = w_project.shape[2] // heads_here
    flat_w = w_project.reshape(channels, -1)
    normed_rows = normalize(pair, ln_gain, ln_shift)
    bias_rows = jnp.einsum("abc,ch->hab", normed_rows, w_bias, preferred_element_type=jnp.float32)
    bias_all = lax.all_gather(bias_rows, "dap", axis=1, tiled=True)
    bias_key_last = jnp.swapaxes(bias_all, 1, 2)
    dap_count = lax.axis_size("dap")
    blocks = pair.reshape(row_count, dap_count, width_n // dap_count, channels)
    packed = project_entries(
        normalize(
            lax.all_to_all(blocks, "dap", split_axis=1, concat_axis=0, tiled=True),
            ln_gain,
            ln_shift,
        ),
        flat_w,
    )
    packed = packed.reshape(width_n, row_count, -1)

    def attend(index):
        column_data = lax.dynamic_index_in_dim(packed, index, 1, keepdims=False)
        pieces = column_data.reshape(width_n, 4, heads_here, head_size)
        scores = jnp.einsum(
            "ihc,khc->hik", pieces[:, 0], pieces[:, 1], preferred_element_type=jnp.float32
        )
        scores = scores * (1.0 / math.sqrt(head_size)) + bias_key_last
        highest = jnp.max(scores, axis=-1, keepdims=True)
        exponent = jnp.exp(scores - highest)
        totals = jnp.sum(exponent, axis=-1)
        weights = exponent.astype(jnp.bfloat16)
        attended = jnp.einsum(
            "hik,khc->ihc", weights, pieces[:, 2], preferred_element_type=jnp.float32
        )
        attended = attended / jnp.swapaxes(totals, 0, 1)[..., None]
        gated_out = (attended * pieces[:, 3].astype(jnp.float32)).astype(jnp.bfloat16)
        return gated_out.reshape(width_n, heads_here * head_size)

    gated_cols = lax.map(attend, jnp.arange(row_count, dtype=jnp.int32))
    returned = lax.all_to_all(
        gated_cols.reshape(row_count, -1), "dap", split_axis=1, concat_axis=0, tiled=True
    )
    returned = returned.reshape(width_n, row_count, heads_here * head_size)
    update = lax.psum_scatter(
        jnp.einsum("jic,cd->ijd", returned, w_out, preferred_element_type=jnp.float32),
        "heads",
        scatter_dimension=0,
        tiled=True,
    )
    return update.astype(jnp.bfloat16)


def solution(mesh):
    in_specs = (
        P("dap", None, None),
        P(),
        P(),
        P(None, None, "heads"),
        P(None, "heads"),
        P("heads", None),
    )
    out_specs = P(("dap", "heads"), None, None)
    return jax.shard_map(local, mesh=mesh, in_specs=in_specs, out_specs=out_specs, check_vma=False)
```

profile of v0, /device:TPU:0, one launch (start us, length us, event | category | flops | bytes accessed | tf_op | source)
XLA Modules:
  0.0 90.6 jit_solution(3977552963952948285)
XLA Ops:
  6.5 0.0 copy-start
  6.5 1.0 %reshape.99 = bf16[6,16,6,128]{3,2,1,0:T(8,128)(2,1)S(1)} reshape(bf16[6,96,128]{2,1,0:T(8,128)(2,1)} %param.8) | data formatting | bytes 294912 | tf_op jit(solution)/shard_map/reshape | solution.py:35
  7.5 0.7 copy.21
  8.2 0.0 copy-start.1
  8.2 7.5 %all-to-all-start = ((bf16[6,16,6,128]{3,2,0,1:T(8,128)(2,1)}), bf16[6,16,6,128]{3,2,0,1:T(8,128)(2,1)S(1)}, u32[]{:S(2)}, u32[]{:S(2)}) async-start(bf16[6,16,6,128]{3,2,0,1:T(8,128)(2,1)} %copy.21), calls=%async_computation | async-start | bytes 393216 | tf_op jit(solution)/shard_map/all_to_all | solution.py:38
  15.8 0.0 reduce-scatter.2.cloned.1.call-start
  15.8 0.0 copy-done.1
  15.8 0.1 convert_reduce_fusion
  16.0 0.3 fusion.18
  16.3 0.0 copy-start.3
  16.3 0.0 copy-start.4
  16.3 0.0 copy-start.5
  16.3 0.6 copy-done.3
  16.9 0.0 copy-done.4
  17.0 0.0 copy-done.5
  17.0 0.3 convolution_bitcast_fusion.3
  17.3 22.0 %all_gather.3 = f32[2,96,96]{2,0,1:T(2,128)S(1)} all-gather(f32[2,6,96]{2,0,1:T(2,128)S(1)} %convolution_bitcast_fusion.3), channel_id=1, replica_groups=mesh['dap'=16,'heads'=2] {'dap'}, dimensions={1}, use_global_device_ids=true | all-gather | bytes 78336 | tf_op jit(solution)/shard_map/all_gather | solution.py:32
  39.3 0.0 all-to-all-done
  39.3 0.2 fusion.9
  39.5 0.3 fusion.12
  39.8 0.3 fusion.15
  40.1 0.0 copy-done
  40.1 0.2 convolution_bitcast_fusion.1
  40.4 0.2 fusion.25
  40.6 0.1 maximum_bitcast_fusion
  40.7 19.9 %while.10 = (s32[]{:T(128)}, bf16[6,96,64]{1,2,0:T(8,128)(2,1)S(1)}, s32[6]{0:T(128)S(1)}, bf16[96,6,256]{2,0,1:T(8,128)(2,1)S(1)}, f32[2,96,96]{1,2,0:T(8,128)S(1)}, /*index=5*/s32[]{:T(128)}, s32[]{:T(128)}, s32[]{:T(128)}) while((s32[]{:T(128)}, bf16[6,96,64]{1,2,0:T(8,128)(2,1)S(1)}, s32[6]{0:T(128)S(1)}, ...), condition=%wide.region_7.8_spmd, body=%wide.region_4.7_spmd.sunk | while | flops 2512517 | bytes 655755 | solution.py:64
  40.7 0.7 dynamic_slice.12
  43.5 0.1 copy.39
  43.6 0.2 fusion.42
  43.9 0.1 fusion.44
  44.0 0.7 dynamic_slice.12
  46.8 0.1 copy.39
  46.9 0.2 fusion.42
  47.2 0.1 fusion.44
  47.4 0.7 dynamic_slice.12
  50.1 0.1 copy.39
  50.2 0.2 fusion.42
  50.5 0.1 fusion.44
  50.7 0.7 dynamic_slice.12
  53.5 0.1 copy.39
  53.6 0.2 fusion.42
  53.8 0.1 fusion.44
  54.0 0.7 dynamic_slice.12
  56.8 0.1 copy.39
  56.9 0.2 fusion.42
  57.2 0.1 fusion.44
  57.3 0.7 dynamic_slice.12
  60.1 0.1 copy.39
  60.2 0.2 fusion.42
  60.5 0.1 fusion.44
  60.7 0.2 copy.26
  60.8 0.2 all_to_all.20
  61.0 10.0 %all_to_all.25 = bf16[6,16,384]{2,0,1:T(8,128)(2,1)S(1)} all-to-all(bf16[6,16,384]{2,0,1:T(8,128)(2,1)S(1)} %copy.27), channel_id=1, replica_groups=mesh['dap'=16,'heads'=2] {'dap'}, dimensions={1} | all-to-all | bytes 147456 | tf_op jit(solution)/shard_map/all_to_all | solution.py:65
  71.0 0.0 copy-start.2
  71.0 0.1 reshape.102
  71.1 0.6 copy-done.2
  71.7 0.9 convolution_bitcast_fusion.2
  72.6 0.0 reduce-scatter.2.cloned.1.call-update
  72.6 9.6 %reduce-scatter.2.cloned.1.call-done = f32[3,96,128]{2,1,0:T(8,128)} async-done(((f32[6,96,128]{2,1,0:T(8,128)}), f32[3,96,128]{2,1,0:T(8,128)}) %reduce-scatter.2.cloned.1.call-update) | async-done | bytes 147472 | tf_op jit(solution)/shard_map/reduce_scatter | solution.py:69
  82.2 1.6 %convert_element_type.59 = bf16[3,96,128]{2,1,0:T(8,128)(2,1)} convert(f32[3,96,128]{2,1,0:T(8,128)} %reduce-scatter.2.cloned.1.call-done) | non-fusion elementwise | flops 36864 | bytes 221184 | tf_op jit(solution)/shard_map/convert_element_type | solution.py:75
  (27 shorter events, 0.5 us)
Async XLA Ops:
  6.5 33.6 %copy-start = (bf16[128,4,64]{0,2,1:T(8,128)(2,1)S(1)}, bf16[128,4,64]{0,2,1:T(8,128)(2,1)}, u32[]{:S(2)}) copy-start(bf16[128,4,64]{0,2,1:T(8,128)(2,1)} %param.11) | copy-start | bytes 196612
  8.2 7.6 %copy-start.1 = (bf16[6,96,128]{2,1,0:T(8,128)(2,1)S(1)}, bf16[6,96,128]{2,1,0:T(8,128)(2,1)}, u32[]{:S(2)}) copy-start(bf16[6,96,128]{2,1,0:T(8,128)(2,1)} %param.8) | copy-start | bytes 442372
  8.2 31.0 %all-to-all-start = ((bf16[6,16,6,128]{3,2,0,1:T(8,128)(2,1)}), bf16[6,16,6,128]{3,2,0,1:T(8,128)(2,1)S(1)}, u32[]{:S(2)}, u32[]{:S(2)}) async-start(bf16[6,16,6,128]{3,2,0,1:T(8,128)(2,1)} %copy.21), calls=%async_computation | async-start | bytes 393216 | tf_op jit(solution)/shard_map/all_to_all | solution.py:38
  15.8 66.4 %reduce-scatter.2.cloned.1.call-start = ((), (), s32[]{:S(2)}) async-start(), calls=%async_computation.3 | async-start | bytes 442368 | tf_op jit(solution)/shard_map/reduce_scatter | solution.py:69
  16.3 0.7 copy-start.3
  16.3 0.7 copy-start.4
  16.3 0.7 copy-start.5
  71.0 0.7 copy-start.2
Sparse Core Ops, SparseCore 0:
  72.7 9.4 reduce-scatter.1
where the time goes:
time: 91.1 us; the launch traced here: 90.6 us
  blocking collectives  32 us (35%)
  between operations  13.6 us (15%)
  loops' own time  12.6 us (14%)
  waiting for transfers between devices  9.61 us (11%)
  local copies, waits for them, and re-layouts  8.24 us (9%)
  starting transfers between devices  7.56 us (8%)
  matrix products  3.72 us (4%)
  other arithmetic  3.32 us (4%)
    all_gather x1, blocking collectives, local(): bias_all = lax.all_gather(bias_rows, 'dap', axis=1, tiled=True)  22 us
    another operation x1, loops' own time, local(): gated_cols = lax.map(attend, jnp.arange(row_count, dtype=jnp.int32))  12.6 us
    all_to_all x1, blocking collectives, local(): lax.all_to_all(gated_cols.reshape(row_count, -1), 'dap', split_axis=1, co...  9.99 us
    reduce_scatter x1, waiting for transfers between devices, local(): lax.psum_scatter(jnp.einsum('jic,cd->ijd', returned, w_out, preferred_ele...  9.59 us
    all_to_all x1, starting transfers between devices, local(): lax.all_to_all(blocks, 'dap', split_axis=1, concat_axis=0, tiled=True)  7.52 us
    dynamic_slice x6, local copies, waits for them, and re-layouts, local(): gated_cols = lax.map(attend, jnp.arange(row_count, dtype=jnp.int32))  4 us
  transfers between devices with their start and end apart: 2, of which 1 were waited for; matrix products, arithmetic and copies ran while one was open for 1% of the time, Pallas kernels for 0%

commit v1 on v0

--- a/solution.py
+++ b/solution.py
@@ -1,9 +1,327 @@
+import functools
 import math
 
 import jax
 import jax.numpy as jnp
 from jax import lax
+from jax.experimental import pallas as pl
+from jax.experimental.pallas import tpu as pltpu
 from jax.sharding import PartitionSpec as P
+
+MESH = pl.DeviceIdType.MESH
+F32 = jnp.float32
+BF16 = jnp.bfloat16
+NT = (((1,), (1,)), ((), ()))
+VMEM_BYTES = 60 * 1024 * 1024
+
+
+def up(size, unit):
+    return -(-size // unit) * unit
+
+
+def nt_dot(left, right):
+    return lax.dot_general(left, right, NT, preferred_element_type=F32)
+
+
+def kernel(
+    dims,
+    pair_hbm,
+    gain_hbm,
+    shift_hbm,
+    bias_hbm,
+    project_hbm,
+    w_out_hbm,
+    out_ref,
+    pair_ref,
+    gain_ref,
+    shift_ref,
+    bias_ref,
+    normed,
+    stage,
+    x_send,
+    x_recv,
+    tokens,
+    w_all,
+    b_pad,
+    b_recv,
+    bias,
+    gated,
+    g_stage,
+    g_send,
+    g_recv,
+    projected,
+    load_sem,
+    w_send_sem,
+    w_recv_sem,
+    x_send_sem,
+    x_recv_sem,
+    b_send_sem,
+    b_recv_sem,
+    g_send_sem,
+    g_recv_sem,
+):
+    n, groups, rows, width, cols, heads, size = dims
+    own_heads = heads // groups
+    inner = own_heads * size
+    devices = n * groups
+    own_rows = rows // groups
+    d = lax.axis_index("dap")
+    g = lax.axis_index("heads")
+    me = g * n + d
+    quad = min(4, n)
+    slabs = n // quad
+    z, r = d // quad, lax.rem(d, quad)
+    planes = [g, 1 - g]
+    dap_at = [lax.rem(d + offset, n) for offset in range(n)]
+    slab_at = [lax.rem(z + back, slabs) * quad for back in range(slabs)]
+    near_at = [lax.rem(r + near, quad) for near in range(quad)]
+
+    barrier = pltpu.get_barrier_semaphore()
+    others = [(k % n, k // n) for k in range(1, devices)]
+    for offset, plane in others:
+        pl.semaphore_signal(
+            barrier, inc=1, device_id=(dap_at[offset], planes[plane]), device_id_type=MESH
+        )
+
+    low_out = 4 * inner
+    loads = [
+        pltpu.make_async_copy(pair_hbm, pair_ref, load_sem.at[0]),
+        pltpu.make_async_copy(gain_hbm, gain_ref, load_sem.at[4]),
+        pltpu.make_async_copy(shift_hbm, shift_ref, load_sem.at[5]),
+    ]
+    w_loads = [
+        pltpu.make_async_copy(bias_hbm, bias_ref, load_sem.at[1]),
+        pltpu.make_async_copy(project_hbm, w_all.at[g, pl.ds(0, low_out)], load_sem.at[2]),
+        pltpu.make_async_copy(w_out_hbm, w_all.at[g, pl.ds(low_out, inner)], load_sem.at[3]),
+    ]
+    for copy in loads + w_loads:
+        copy.start()
+
+    for copy in loads:
+        copy.wait()
+    gain = gain_ref[...]
+    shift = shift_ref[...]
+    for a in range(rows):
+        values = pair_ref[a].astype(F32)
+        average = jnp.mean(values, axis=-1, keepdims=True)
+        centred = values - average
+        variance = jnp.mean(centred * centred, axis=-1, keepdims=True)
+        normed[a * width : (a + 1) * width, :] = (
+            centred * lax.rsqrt(variance + 1e-05) * gain + shift
+        )
+
+    x_rows = x_send.shape[1]
+    for a in range(rows):
+        for c in range(cols):
+            start = pl.multiple_of(a * width + c * devices + g * n, 8)
+            stage[pl.ds(a * cols + c, n, x_rows), :] = normed[pl.ds(start, n), :]
+    x_send[...] = stage[...].reshape(n, x_rows, -1).astype(BF16)
+
+    w_loads[0].wait()
+    b_pad[0:own_heads, :] = bias_ref[...]
+    w_bias = b_pad[...]
+    for a in range(rows):
+        part = nt_dot(w_bias, normed[a * width : (a + 1) * width, :].astype(BF16))
+        for h in range(own_heads):
+            row = h * rows + a
+            b_recv[d, g, row : row + 1, 0:width] = part[h : h + 1]
+    for copy in w_loads[1:]:
+        copy.wait()
+
+    pl.semaphore_wait(barrier, devices - 1)
+
+    def send(src, dst, send_sem, recv_sem, other, plane=g):
+        copy = pltpu.make_async_remote_copy(
+            src_ref=src,
+            dst_ref=dst,
+            send_sem=send_sem,
+            recv_sem=recv_sem,
+            device_id=(other, plane),
+            device_id_type=MESH,
+        )
+        copy.start()
+        return copy
+
+    def drain(ref, sem):
+        pltpu.make_async_copy(ref, ref, sem).wait()
+
+    b_used = own_heads * rows
+    own_bias = b_recv.at[d, g, pl.ds(0, b_used)]
+    first = [(back, plane) for plane in range(groups) for back in range(slabs)][1:]
+    across = {}
+    for back, plane in first:
+        k = back * groups + plane
+        across[back, plane] = send(
+            own_bias, own_bias, b_send_sem.at[0], b_recv_sem.at[k], slab_at[back] + r, planes[plane]
+        )
+
+    far = [near + back * quad for back in range(1, slabs) for near in range(quad)]
+    for offset in far + list(range(1, quad)):
+        other = slab_at[offset // quad] + near_at[offset % quad]
+        send(x_send.at[other], x_recv.at[d], x_send_sem, x_recv_sem, other)
+    own_w = w_all.at[g]
+    w_copy = send(own_w, own_w, w_send_sem, w_recv_sem, d, planes[1])
+    x_recv[d] = x_send[d]
+
+    for back in range(slabs):
+        for plane in range(groups):
+            if back or plane:
+                across[back, plane].wait_recv()
+        block = slab_at[(slabs - back) % slabs] + r
+        both = b_recv.at[block, :, pl.ds(0, b_used)]
+        for near in range(1, quad):
+            send(both, both, b_send_sem.at[1], b_recv_sem.at[0], slab_at[0] + near_at[near])
+
+    drain(x_recv.at[pl.ds(0, n - 1)], x_recv_sem)
+    stage[...] = x_recv[...].reshape(n * x_rows, -1).astype(F32)
+    for a in range(rows):
+        for c in range(cols):
+            tokens[pl.ds(c * width + a, n, rows), :] = stage[pl.ds(a * cols + c, n, x_rows), :]
+    entries = tokens[...].astype(BF16)
+
+    w_copy.wait_recv()
+
+    def weight(t):
+        low = t * inner
+        return jnp.concatenate([w_all[k, low : low + inner, :] for k in range(groups)], axis=0)
+
+    queries = nt_dot(entries, weight(0)).astype(BF16)
+    keys = nt_dot(entries, weight(1)).astype(BF16)
+    w_value, w_gate = weight(2), weight(3)
+    lane = lax.broadcasted_iota(jnp.int32, (width, heads * size), 1) // size
+    scores, values, gating = [], [], []
+    for c in range(cols):
+        part = slice(c * width, (c + 1) * width)
+        key = keys[part]
+        stacked = jnp.concatenate(
+            [jnp.where(lane == h, key, jnp.zeros_like(key)) for h in range(heads)], axis=0
+        )
+        scores.append(nt_dot(stacked, queries[part]))
+        values.append(nt_dot(w_value, entries[part]).astype(BF16))
+        gating.append(jax.nn.sigmoid(nt_dot(w_gate, entries[part])).astype(BF16).astype(F32))
+
+    passed = slabs * (quad - 1)
+    drain(b_recv.at[pl.ds(0, passed), :, pl.ds(0, b_used)], b_recv_sem.at[0])
+    b_rows = b_recv.shape[2]
+    gathered = b_recv.reshape(n * groups * b_rows, 128)
+    for h in range(heads):
+        for a in range(rows):
+            first_row = h // own_heads * b_rows + h % own_heads * rows + a
+            bias[pl.ds(h * width + a, n, rows), :] = gathered[
+                pl.ds(first_row, n, groups * b_rows), :
+            ]
+
+    scale = 1.0 / math.sqrt(size)
+    for c in range(cols):
+        parts = []
+        for h in range(heads):
+            part = slice(h * width, (h + 1) * width)
+            score = scores[c][part] * scale + bias[part, 0:width]
+            exponent = jnp.exp(score - jnp.max(score, axis=0, keepdims=True))
+            total = jnp.sum(exponent, axis=0, keepdims=True)
+            head = slice(h * size, (h + 1) * size)
+            attended = jnp.dot(values[c][head], exponent.astype(BF16), preferred_element_type=F32)
+            parts.append(attended / total * gating[c][head])
+        gated[c * width : (c + 1) * width, :] = jnp.concatenate(parts, axis=0).T
+
+    g_rows = g_send.shape[1]
+    for i in range(own_rows):
+        for c in range(cols):
+            g_stage[pl.ds(i * cols + c, devices, g_rows), :] = gated[
+                pl.ds(c * width + i, devices, own_rows), :
+            ]
+    g_send[...] = g_stage[...].reshape(devices, g_rows, -1).astype(BF16)
+
+    for offset, plane in sorted(others, key=lambda o: -min(o[0], n - o[0])):
+        other_d, other_g = dap_at[offset], planes[plane]
+        send(
+            g_send.at[other_d * groups + other_g],
+            g_recv.at[me],
+            g_send_sem,
+            g_recv_sem,
+            other_d,
+            other_g,
+        )
+    g_recv[me] = g_send[d * groups + g]
+    drain(b_recv.at[pl.ds(0, len(first)), 0, pl.ds(0, b_used)], b_send_sem.at[0])
+    drain(b_recv.at[pl.ds(0, passed), :, pl.ds(0, b_used)], b_send_sem.at[1])
+    drain(x_send.at[pl.ds(0, n - 1)], x_send_sem)
+    w_copy.wait_send()
+    drain(g_send.at[pl.ds(0, devices - 1)], g_send_sem)
+    w_out = jnp.concatenate([w_all[k, low_out : low_out + inner, :] for k in range(groups)], axis=0)
+    drain(g_recv.at[pl.ds(0, devices - 1)], g_recv_sem)
+    projected[...] = jnp.dot(
+        g_recv[...].reshape(devices * g_rows, -1), w_out, preferred_element_type=F32
+    )
+    for i in range(own_rows):
+        for c in range(cols):
+            out_ref[i, c * devices : (c + 1) * devices, :] = projected[
+                pl.ds(i * cols + c, devices, g_rows), :
+            ].astype(BF16)
+
+
+def fused(n, groups, pair, ln_gain, ln_shift, w_project, w_bias, w_out):
+    rows, width, channels = pair.shape
+    own_heads = w_bias.shape[1]
+    heads = own_heads * groups
+    size = w_project.shape[2] // own_heads
+    devices = n * groups
+    cols = width // devices
+    own_rows = rows // groups
+    inner = own_heads * size
+    w_rows = 5 * inner
+    b_rows = up(own_heads * rows, 8)
+    x_rows = up(rows * cols, 16)
+    g_rows = up(own_rows * cols, 16)
+    dims = (n, groups, rows, width, cols, heads, size)
+    vmem = pl.BlockSpec(memory_space=pltpu.VMEM)
+    hbm = pl.BlockSpec(memory_space=pl.ANY)
+    sems = pltpu.SemaphoreType.DMA
+    return pl.pallas_call(
+        functools.partial(kernel, dims),
+        out_shape=pltpu.VMEM((own_rows, width, channels), BF16),
+        in_specs=[hbm] * 6,
+        out_specs=vmem,
+        scratch_shapes=[
+            pltpu.VMEM((rows, width, channels), BF16),
+            pltpu.VMEM((1, channels), F32),
+            pltpu.VMEM((1, channels), F32),
+            pltpu.VMEM((own_heads, channels), BF16),
+            pltpu.VMEM((rows * width, channels), F32),
+            pltpu.VMEM((n * x_rows, channels), F32),
+            pltpu.VMEM((n, x_rows, channels), BF16),
+            pltpu.VMEM((n, x_rows, channels), BF16),
+            pltpu.VMEM((cols * width, channels), F32),
+            pltpu.VMEM((groups, w_rows, channels), BF16),
+            pltpu.VMEM((16, channels), BF16),
+            pltpu.VMEM((n, groups, b_rows, 128), F32),
+            pltpu.VMEM((heads * width, 128), F32),
+            pltpu.VMEM((cols * width, heads * size), F32),
+            pltpu.VMEM((devices * g_rows, heads * size), F32),
+            pltpu.VMEM((devices, g_rows, heads * size), BF16),
+            pltpu.VMEM((devices, g_rows, heads * size), BF16),
+            pltpu.VMEM((devices * g_rows, channels), F32),
+            sems((6,)),
+            sems(()),
+            sems(()),
+            sems(()),
+            sems(()),
+            sems((2,)),
+            sems((n // min(4, n) * groups,)),
+            sems(()),
+            sems(()),
+        ],
+        compiler_params=pltpu.CompilerParams(
+            collective_id=0, has_side_effects=True, vmem_limit_bytes=VMEM_BYTES
+        ),
+    )(
+        pair,
+        ln_gain.reshape(1, -1),
+        ln_shift.reshape(1, -1),
+        w_bias.T,
+        jnp.transpose(w_project, (1, 2, 0)).reshape(-1, channels),
+        w_out,
+    )
 
 
 def normalize(pair, ln_gain, ln_shift):
@@ -75,7 +393,30 @@
     return update.astype(jnp.bfloat16)
 
 
+def fits(mesh, pair, w_bias):
+    n, groups = mesh.shape["dap"], mesh.shape["heads"]
+    rows, width, channels = pair.shape
+    devices = n * groups
+    heads = w_bias.shape[1] * groups
+    return (
+        groups == 2
+        and channels == 128
+        and width <= 128
+        and width % devices == 0
+        and width % 32 == 0
+        and n % 8 == 0
+        and rows % groups == 0
+    )
+
+
 def solution(mesh):
+    n, groups = mesh.shape["dap"], mesh.shape["heads"]
+
+    def run(pair, ln_gain, ln_shift, w_project, w_bias, w_out):
+        if fits(mesh, pair, w_bias):
+            return fused(n, groups, pair, ln_gain, ln_shift, w_project, w_bias, w_out)
+        return local(pair, ln_gain, ln_shift, w_project, w_bias, w_out)
+
     in_specs = (
         P("dap", None, None),
         P(),
@@ -85,4 +426,4 @@
         P("heads", None),
     )
     out_specs = P(("dap", "heads"), None, None)
-    return jax.shard_map(local, mesh=mesh, in_specs=in_specs, out_specs=out_specs, check_vma=False)
+    return jax.shard_map(run, mesh=mesh, in_specs=in_specs, out_specs=out_specs, check_vma=False)

time: 91.1 us -> 21.9 us (0.24)
  blocking collectives: 32 us -> 0 us
  Pallas kernels: 0 us -> 21.2 us
  between operations: 13.6 us -> 0.01 us
  loops' own time: 12.6 us -> 0 us
  waiting for transfers between devices: 9.61 us -> 0 us
  local copies, waits for them, and re-layouts: 8.24 us -> 0.64 us
  starting transfers between devices: 7.56 us -> 0 us
  matrix products: 3.72 us -> 0 us
  other arithmetic: 3.32 us -> 0 us
    all_gather x1 -> x0, blocking collectives: 22 us -> none  [local(): bias_all = lax.all_gather(bias_rows, 'dap', axis=1, tiled=True)]
    pallas_call x0 -> x1, Pallas kernels: none -> 21.2 us  [fused(): pl.pallas_call(functools.partial(kernel, dims), out_shape=pltpu.VMEM((own...]
    another operation x1 -> x0, loops' own time: 12.6 us -> none  [local(): gated_cols = lax.map(attend, jnp.arange(row_count, dtype=jnp.int32))]
    all_to_all x1 -> x0, blocking collectives: 9.99 us -> none  [local(): lax.all_to_all(gated_cols.reshape(row_count, -1), 'dap', split_axis=1, co...]
    reduce_scatter x1 -> x0, waiting for transfers between devices: 9.59 us -> none  [local(): lax.psum_scatter(jnp.einsum('jic,cd->ijd', returned, w_out, preferred_ele...]
    all_to_all x1 -> x0, starting transfers between devices: 7.52 us -> none  [local(): lax.all_to_all(blocks, 'dap', split_axis=1, concat_axis=0, tiled=True)]
    dynamic_slice x18 -> x0, local copies, waits for them, and re-layouts: 4.73 us -> none  [the longest x6 4 us: local(): gated_cols = lax.map(attend, jnp.arange(row_count, dtype=jnp.int32))]
    dot_general x15 -> x0, matrix products: 3.72 us -> none  [the longest x6 1.41 us: attend(): jnp.einsum('ihc,khc->hik', pieces[:, 0], pieces[:, 1], preferred_element_...]
  transfers between devices with their start and end apart: 2 -> 0, of which waited for: 1 -> 0; matrix products, arithmetic and copies ran while one was open for 1% -> 0% of each run, Pallas kernels for 0% -> 0%
where the time goes in v1:
time: 21.9 us; the launch traced here: 21.8 us
  Pallas kernels  21.2 us (97%)
  local copies, waits for them, and re-layouts  0.64 us (3%)
    pallas_call x1, Pallas kernels, fused(): pl.pallas_call(functools.partial(kernel, dims), out_shape=pltpu.VMEM((own...  21.2 us
    unnamed x1, local copies, waits for them, and re-layouts  0.64 us

profile of v1, /device:TPU:0, one launch (start us, length us, event | category | flops | bytes accessed | tf_op | source)
XLA Modules:
  0.0 21.8 jit_solution(4991812432283456299)
XLA Ops:
  0.0 21.2 %shard_map.64 = bf16[3,96,128]{2,1,0:T(8,128)(2,1)S(1)} custom-call(bf16[6,96,128]{2,1,0:T(8,128)(2,1)} %pair_hbm.1, f32[1,128]{1,0:T(1,128)} %bitcast.7, f32[1,128]{1,0:T(1,128)} %bitcast.8, bf16[2,128]{1,0:T(2,128)(2,1)} %bitcast.9, bf16[256,128]{1,0:T(8,128)(2,1)} %bitcast.6, bf16[64,128]{1,0:T(8,128)(2,1)} %w_out_hbm.1), custom_call_target="tpu_custom_call" | custom-call | tf_op jit(solution)/shard_map/pallas_call | solution.py:280
  21.2 0.6 %copy.8 = bf16[3,96,128]{2,1,0:T(8,128)(2,1)} copy(bf16[3,96,128]{2,1,0:T(8,128)(2,1)S(1)} %shard_map.64) | data formatting | bytes 147456

commit v2 on v1

--- a/solution.py
+++ b/solution.py
@@ -68,20 +68,8 @@
     d = lax.axis_index("dap")
     g = lax.axis_index("heads")
     me = g * n + d
-    quad = min(4, n)
-    slabs = n // quad
-    z, r = d // quad, lax.rem(d, quad)
     planes = [g, 1 - g]
     dap_at = [lax.rem(d + offset, n) for offset in range(n)]
-    slab_at = [lax.rem(z + back, slabs) * quad for back in range(slabs)]
-    near_at = [lax.rem(r + near, quad) for near in range(quad)]
-
-    barrier = pltpu.get_barrier_semaphore()
-    others = [(k % n, k // n) for k in range(1, devices)]
-    for offset, plane in others:
-        pl.semaphore_signal(
-            barrier, inc=1, device_id=(dap_at[offset], planes[plane]), device_id_type=MESH
-        )
 
     low_out = 4 * inner
     loads = [
@@ -97,6 +85,13 @@
     for copy in loads + w_loads:
         copy.start()
 
+    barrier = pltpu.get_barrier_semaphore()
+    others = [(k % n, k // n) for k in range(1, devices)]
+    for offset, plane in others:
+        pl.semaphore_signal(
+            barrier, inc=1, device_id=(dap_at[offset], planes[plane]), device_id_type=MESH
+        )
+
     for copy in loads:
         copy.wait()
     gain = gain_ref[...]
@@ -124,7 +119,7 @@
         part = nt_dot(w_bias, normed[a * width : (a + 1) * width, :].astype(BF16))
         for h in range(own_heads):
             row = h * rows + a
-            b_recv[d, g, row : row + 1, 0:width] = part[h : h + 1]
+            b_recv[d * groups + g, row : row + 1, 0:width] = part[h : h + 1]
     for copy in w_loads[1:]:
         copy.wait()
 
@@ -145,32 +140,20 @@
     def drain(ref, sem):
         pltpu.make_async_copy(ref, ref, sem).wait()
 
+    def drain_bias(sem):
+        drain(b_recv.at[pl.ds(0, devices - 1), pl.ds(0, b_used)], sem)
+
+    far = sorted(others, key=lambda o: -min(o[0], n - o[0]))
+    for offset, plane in far:
+        if plane == 0:
+            send(x_send.at[dap_at[offset]], x_recv.at[d], x_send_sem, x_recv_sem, dap_at[offset])
     b_used = own_heads * rows
-    own_bias = b_recv.at[d, g, pl.ds(0, b_used)]
-    first = [(back, plane) for plane in range(groups) for back in range(slabs)][1:]
-    across = {}
-    for back, plane in first:
-        k = back * groups + plane
-        across[back, plane] = send(
-            own_bias, own_bias, b_send_sem.at[0], b_recv_sem.at[k], slab_at[back] + r, planes[plane]
-        )
-
-    far = [near + back * quad for back in range(1, slabs) for near in range(quad)]
-    for offset in far + list(range(1, quad)):
-        other = slab_at[offset // quad] + near_at[offset % quad]
-        send(x_send.at[other], x_recv.at[d], x_send_sem, x_recv_sem, other)
+    own_bias = b_recv.at[d * groups + g, pl.ds(0, b_used)]
+    for offset, plane in far:
+        send(own_bias, own_bias, b_send_sem, b_recv_sem, dap_at[offset], planes[plane])
     own_w = w_all.at[g]
     w_copy = send(own_w, own_w, w_send_sem, w_recv_sem, d, planes[1])
     x_recv[d] = x_send[d]
-
-    for back in range(slabs):
-        for plane in range(groups):
-            if back or plane:
-                across[back, plane].wait_recv()
-        block = slab_at[(slabs - back) % slabs] + r
-        both = b_recv.at[block, :, pl.ds(0, b_used)]
-        for near in range(1, quad):
-            send(both, both, b_send_sem.at[1], b_recv_sem.at[0], slab_at[0] + near_at[near])
 
     drain(x_recv.at[pl.ds(0, n - 1)], x_recv_sem)
     stage[...] = x_recv[...].reshape(n * x_rows, -1).astype(F32)
@@ -200,9 +183,8 @@
         values.append(nt_dot(w_value, entries[part]).astype(BF16))
         gating.append(jax.nn.sigmoid(nt_dot(w_gate, entries[part])).astype(BF16).astype(F32))
 
-    passed = slabs * (quad - 1)
-    drain(b_recv.at[pl.ds(0, passed), :, pl.ds(0, b_used)], b_recv_sem.at[0])
-    b_rows = b_recv.shape[2]
+    drain_bias(b_recv_sem)
+    b_rows = b_recv.shape[1]
     gathered = b_recv.reshape(n * groups * b_rows, 128)
     for h in range(heads):
         for a in range(rows):
@@ -232,7 +214,7 @@
             ]
     g_send[...] = g_stage[...].reshape(devices, g_rows, -1).astype(BF16)
 
-    for offset, plane in sorted(others, key=lambda o: -min(o[0], n - o[0])):
+    for offset, plane in far:
         other_d, other_g = dap_at[offset], planes[plane]
         send(
             g_send.at[other_d * groups + other_g],
@@ -243,8 +225,7 @@
             other_g,
         )
     g_recv[me] = g_send[d * groups + g]
-    drain(b_recv.at[pl.ds(0, len(first)), 0, pl.ds(0, b_used)], b_send_sem.at[0])
-    drain(b_recv.at[pl.ds(0, passed), :, pl.ds(0, b_used)], b_send_sem.at[1])
+    drain_bias(b_send_sem)
     drain(x_send.at[pl.ds(0, n - 1)], x_send_sem)
     w_copy.wait_send()
     drain(g_send.at[pl.ds(0, devices - 1)], g_send_sem)
@@ -294,7 +275,7 @@
             pltpu.VMEM((cols * width, channels), F32),
             pltpu.VMEM((groups, w_rows, channels), BF16),
             pltpu.VMEM((16, channels), BF16),
-            pltpu.VMEM((n, groups, b_rows, 128), F32),
+            pltpu.VMEM((devices, b_rows, 128), F32),
             pltpu.VMEM((heads * width, 128), F32),
             pltpu.VMEM((cols * width, heads * size), F32),
             pltpu.VMEM((devices * g_rows, heads * size), F32),
@@ -306,8 +287,8 @@
             sems(()),
             sems(()),
             sems(()),
-            sems((2,)),
-            sems((n // min(4, n) * groups,)),
+            sems(()),
+            sems(()),
             sems(()),
             sems(()),
         ],

time: 21.9 us -> 24.2 us (1.11)
  Pallas kernels: 21.2 us -> 23.4 us
    pallas_call x1, Pallas kernels: 21.2 us -> 23.4 us  [fused(): pl.pallas_call(functools.partial(kernel, dims), out_shape=pltpu.VMEM((own...]
where the time goes in v2:
time: 24.2 us; the launch traced here: 24 us
  Pallas kernels  23.4 us (97%)
  local copies, waits for them, and re-layouts  0.64 us (3%)
    pallas_call x1, Pallas kernels, fused(): pl.pallas_call(functools.partial(kernel, dims), out_shape=pltpu.VMEM((own...  23.4 us
    unnamed x1, local copies, waits for them, and re-layouts  0.64 us

profile of v2, /device:TPU:0, one launch (start us, length us, event | category | flops | bytes accessed | tf_op | source)
XLA Modules:
  0.0 24.0 jit_solution(1348914660383865879)
XLA Ops:
  0.0 23.4 %shard_map.64 = bf16[3,96,128]{2,1,0:T(8,128)(2,1)S(1)} custom-call(bf16[6,96,128]{2,1,0:T(8,128)(2,1)} %pair_hbm.1, f32[1,128]{1,0:T(1,128)} %bitcast.7, f32[1,128]{1,0:T(1,128)} %bitcast.8, bf16[2,128]{1,0:T(2,128)(2,1)} %bitcast.9, bf16[256,128]{1,0:T(8,128)(2,1)} %bitcast.6, bf16[64,128]{1,0:T(8,128)(2,1)} %w_out_hbm.1), custom_call_target="tpu_custom_call" | custom-call | tf_op jit(solution)/shard_map/pallas_call | solution.py:261
  23.4 0.6 %copy.8 = bf16[3,96,128]{2,1,0:T(8,128)(2,1)} copy(bf16[3,96,128]{2,1,0:T(8,128)(2,1)S(1)} %shard_map.64) | data formatting | bytes 147456

commit v3 on v1

--- a/solution.py
+++ b/solution.py
@@ -76,13 +76,6 @@
     slab_at = [lax.rem(z + back, slabs) * quad for back in range(slabs)]
     near_at = [lax.rem(r + near, quad) for near in range(quad)]
 
-    barrier = pltpu.get_barrier_semaphore()
-    others = [(k % n, k // n) for k in range(1, devices)]
-    for offset, plane in others:
-        pl.semaphore_signal(
-            barrier, inc=1, device_id=(dap_at[offset], planes[plane]), device_id_type=MESH
-        )
-
     low_out = 4 * inner
     loads = [
         pltpu.make_async_copy(pair_hbm, pair_ref, load_sem.at[0]),
@@ -97,6 +90,13 @@
     for copy in loads + w_loads:
         copy.start()
 
+    barrier = pltpu.get_barrier_semaphore()
+    others = [(k % n, k // n) for k in range(1, devices)]
+    for offset, plane in others:
+        pl.semaphore_signal(
+            barrier, inc=1, device_id=(dap_at[offset], planes[plane]), device_id_type=MESH
+        )
+
     for copy in loads:
         copy.wait()
     gain = gain_ref[...]
@@ -110,12 +110,13 @@
             centred * lax.rsqrt(variance + 1e-05) * gain + shift
         )
 
-    x_rows = x_send.shape[1]
+    x_used = x_send.shape[1]
+    x_rows = up(x_used, 8)
     for a in range(rows):
         for c in range(cols):
             start = pl.multiple_of(a * width + c * devices + g * n, 8)
             stage[pl.ds(a * cols + c, n, x_rows), :] = normed[pl.ds(start, n), :]
-    x_send[...] = stage[...].reshape(n, x_rows, -1).astype(BF16)
+    x_send[...] = stage[...].reshape(n, x_rows, -1)[:, :x_used].astype(BF16)
 
     w_loads[0].wait()
     b_pad[0:own_heads, :] = bias_ref[...]
@@ -173,7 +174,8 @@
             send(both, both, b_send_sem.at[1], b_recv_sem.at[0], slab_at[0] + near_at[near])
 
     drain(x_recv.at[pl.ds(0, n - 1)], x_recv_sem)
-    stage[...] = x_recv[...].reshape(n * x_rows, -1).astype(F32)
+    for k in range(n):
+        stage[k * x_rows : k * x_rows + x_used, :] = x_recv[k].astype(F32)
     for a in range(rows):
         for c in range(cols):
             tokens[pl.ds(c * width + a, n, rows), :] = stage[pl.ds(a * cols + c, n, x_rows), :]
@@ -224,13 +226,14 @@
             parts.append(attended / total * gating[c][head])
         gated[c * width : (c + 1) * width, :] = jnp.concatenate(parts, axis=0).T
 
-    g_rows = g_send.shape[1]
+    g_used = g_send.shape[1]
+    g_rows = up(g_used, 8)
     for i in range(own_rows):
         for c in range(cols):
             g_stage[pl.ds(i * cols + c, devices, g_rows), :] = gated[
                 pl.ds(c * width + i, devices, own_rows), :
             ]
-    g_send[...] = g_stage[...].reshape(devices, g_rows, -1).astype(BF16)
+    g_send[...] = g_stage[...].reshape(devices, g_rows, -1)[:, :g_used].astype(BF16)
 
     for offset, plane in sorted(others, key=lambda o: -min(o[0], n - o[0])):
         other_d, other_g = dap_at[offset], planes[plane]
@@ -250,9 +253,9 @@
     drain(g_send.at[pl.ds(0, devices - 1)], g_send_sem)
     w_out = jnp.concatenate([w_all[k, low_out : low_out + inner, :] for k in range(groups)], axis=0)
     drain(g_recv.at[pl.ds(0, devices - 1)], g_recv_sem)
-    projected[...] = jnp.dot(
-        g_recv[...].reshape(devices * g_rows, -1), w_out, preferred_element_type=F32
-    )
+    for k in range(devices):
+        g_stage[k * g_rows : k * g_rows + g_used, :] = g_recv[k].astype(F32)
+    projected[...] = jnp.dot(g_stage[...].astype(BF16), w_out, preferred_element_type=F32)
     for i in range(own_rows):
         for c in range(cols):
             out_ref[i, c * devices : (c + 1) * devices, :] = projected[
@@ -271,8 +274,10 @@
     inner = own_heads * size
     w_rows = 5 * inner
     b_rows = up(own_heads * rows, 8)
-    x_rows = up(rows * cols, 16)
-    g_rows = up(own_rows * cols, 16)
+    x_used = up(rows * cols, 2)
+    x_rows = up(x_used, 8)
+    g_used = up(own_rows * cols, 2)
+    g_rows = up(g_used, 8)
     dims = (n, groups, rows, width, cols, heads, size)
     vmem = pl.BlockSpec(memory_space=pltpu.VMEM)
     hbm = pl.BlockSpec(memory_space=pl.ANY)
@@ -289,8 +294,8 @@
             pltpu.VMEM((own_heads, channels), BF16),
             pltpu.VMEM((rows * width, channels), F32),
             pltpu.VMEM((n * x_rows, channels), F32),
-            pltpu.VMEM((n, x_rows, channels), BF16),
-            pltpu.VMEM((n, x_rows, channels), BF16),
+            pltpu.VMEM((n, x_used, channels), BF16),
+            pltpu.VMEM((n, x_used, channels), BF16),
             pltpu.VMEM((cols * width, channels), F32),
             pltpu.VMEM((groups, w_rows, channels), BF16),
             pltpu.VMEM((16, channels), BF16),
@@ -298,8 +303,8 @@
             pltpu.VMEM((heads * width, 128), F32),
             pltpu.VMEM((cols * width, heads * size), F32),
             pltpu.VMEM((devices * g_rows, heads * size), F32),
-            pltpu.VMEM((devices, g_rows, heads * size), BF16),
-            pltpu.VMEM((devices, g_rows, heads * size), BF16),
+            pltpu.VMEM((devices, g_used, heads * size), BF16),
+            pltpu.VMEM((devices, g_used, heads * size), BF16),
             pltpu.VMEM((devices * g_rows, channels), F32),
             sems((6,)),
             sems(()),

time: 21.9 us -> 22 us (level)
  no operation moved by 1% of the time
where the time goes in v3:
time: 22 us; the launch traced here: 21.9 us
  Pallas kernels  21.2 us (96%)
  local copies, waits for them, and re-layouts  0.64 us (3%)
    pallas_call x1, Pallas kernels, fused(): pl.pallas_call(functools.partial(kernel, dims), out_shape=pltpu.VMEM((own...  21.2 us
    unnamed x1, local copies, waits for them, and re-layouts  0.64 us

profile of v3, /device:TPU:0, one launch (start us, length us, event | category | flops | bytes accessed | tf_op | source)
XLA Modules:
  0.0 21.9 jit_solution(169166581016648739)
XLA Ops:
  0.0 21.2 %shard_map.64 = bf16[3,96,128]{2,1,0:T(8,128)(2,1)S(1)} custom-call(bf16[6,96,128]{2,1,0:T(8,128)(2,1)} %pair_hbm.1, f32[1,128]{1,0:T(1,128)} %bitcast.7, f32[1,128]{1,0:T(1,128)} %bitcast.8, bf16[2,128]{1,0:T(2,128)(2,1)} %bitcast.9, bf16[256,128]{1,0:T(8,128)(2,1)} %bitcast.6, bf16[64,128]{1,0:T(8,128)(2,1)} %w_out_hbm.1), custom_call_target="tpu_custom_call" | custom-call | tf_op jit(solution)/shard_map/pallas_call | solution.py:285
  21.2 0.6 %copy.8 = bf16[3,96,128]{2,1,0:T(8,128)(2,1)} copy(bf16[3,96,128]{2,1,0:T(8,128)(2,1)S(1)} %shard_map.64) | data formatting | bytes 147456

commit v4 on v1

--- a/solution.py
+++ b/solution.py
@@ -76,13 +76,6 @@
     slab_at = [lax.rem(z + back, slabs) * quad for back in range(slabs)]
     near_at = [lax.rem(r + near, quad) for near in range(quad)]
 
-    barrier = pltpu.get_barrier_semaphore()
-    others = [(k % n, k // n) for k in range(1, devices)]
-    for offset, plane in others:
-        pl.semaphore_signal(
-            barrier, inc=1, device_id=(dap_at[offset], planes[plane]), device_id_type=MESH
-        )
-
     low_out = 4 * inner
     loads = [
         pltpu.make_async_copy(pair_hbm, pair_ref, load_sem.at[0]),
@@ -97,6 +90,13 @@
     for copy in loads + w_loads:
         copy.start()
 
+    barrier = pltpu.get_barrier_semaphore()
+    others = [(k % n, k // n) for k in range(1, devices)]
+    for offset, plane in others:
+        pl.semaphore_signal(
+            barrier, inc=1, device_id=(dap_at[offset], planes[plane]), device_id_type=MESH
+        )
+
     for copy in loads:
         copy.wait()
     gain = gain_ref[...]
@@ -145,8 +145,7 @@
     def drain(ref, sem):
         pltpu.make_async_copy(ref, ref, sem).wait()
 
-    b_used = own_heads * rows
-    own_bias = b_recv.at[d, g, pl.ds(0, b_used)]
+    own_bias = b_recv.at[d, g]
     first = [(back, plane) for plane in range(groups) for back in range(slabs)][1:]
     across = {}
     for back, plane in first:
@@ -168,7 +167,7 @@
             if back or plane:
                 across[back, plane].wait_recv()
         block = slab_at[(slabs - back) % slabs] + r
-        both = b_recv.at[block, :, pl.ds(0, b_used)]
+        both = b_recv.at[block]
         for near in range(1, quad):
             send(both, both, b_send_sem.at[1], b_recv_sem.at[0], slab_at[0] + near_at[near])
 
@@ -201,7 +200,7 @@
         gating.append(jax.nn.sigmoid(nt_dot(w_gate, entries[part])).astype(BF16).astype(F32))
 
     passed = slabs * (quad - 1)
-    drain(b_recv.at[pl.ds(0, passed), :, pl.ds(0, b_used)], b_recv_sem.at[0])
+    drain(b_recv.at[pl.ds(0, passed)], b_recv_sem.at[0])
     b_rows = b_recv.shape[2]
     gathered = b_recv.reshape(n * groups * b_rows, 128)
     for h in range(heads):
@@ -243,8 +242,8 @@
             other_g,
         )
     g_recv[me] = g_send[d * groups + g]
-    drain(b_recv.at[pl.ds(0, len(first)), 0, pl.ds(0, b_used)], b_send_sem.at[0])
-    drain(b_recv.at[pl.ds(0, passed), :, pl.ds(0, b_used)], b_send_sem.at[1])
+    drain(b_recv.at[pl.ds(0, len(first)), 0], b_send_sem.at[0])
+    drain(b_recv.at[pl.ds(0, passed)], b_send_sem.at[1])
     drain(x_send.at[pl.ds(0, n - 1)], x_send_sem)
     w_copy.wait_send()
     drain(g_send.at[pl.ds(0, devices - 1)], g_send_sem)

time: 21.9 us -> 22.3 us (1.018)
  Pallas kernels: 21.2 us -> 21.5 us
    pallas_call x1, Pallas kernels: 21.2 us -> 21.5 us  [fused(): pl.pallas_call(functools.partial(kernel, dims), out_shape=pltpu.VMEM((own...]
where the time goes in v4:
time: 22.3 us; the launch traced here: 22.2 us
  Pallas kernels  21.5 us (96%)
  local copies, waits for them, and re-layouts  0.64 us (3%)
    pallas_call x1, Pallas kernels, fused(): pl.pallas_call(functools.partial(kernel, dims), out_shape=pltpu.VMEM((own...  21.5 us
    unnamed x1, local copies, waits for them, and re-layouts  0.64 us

profile of v4, /device:TPU:0, one launch (start us, length us, event | category | flops | bytes accessed | tf_op | source)
XLA Modules:
  0.0 22.2 jit_solution(1293769020021078488)
XLA Ops:
  0.0 21.5 %shard_map.64 = bf16[3,96,128]{2,1,0:T(8,128)(2,1)S(1)} custom-call(bf16[6,96,128]{2,1,0:T(8,128)(2,1)} %pair_hbm.1, f32[1,128]{1,0:T(1,128)} %bitcast.7, f32[1,128]{1,0:T(1,128)} %bitcast.8, bf16[2,128]{1,0:T(2,128)(2,1)} %bitcast.9, bf16[256,128]{1,0:T(8,128)(2,1)} %bitcast.6, bf16[64,128]{1,0:T(8,128)(2,1)} %w_out_hbm.1), custom_call_target="tpu_custom_call" | custom-call | tf_op jit(solution)/shard_map/pallas_call | solution.py:279
  21.5 0.6 %copy.8 = bf16[3,96,128]{2,1,0:T(8,128)(2,1)} copy(bf16[3,96,128]{2,1,0:T(8,128)(2,1)S(1)} %shard_map.64) | data formatting | bytes 147456

commit v5 on v4

--- a/solution.py
+++ b/solution.py
@@ -106,25 +106,27 @@
         average = jnp.mean(values, axis=-1, keepdims=True)
         centred = values - average
         variance = jnp.mean(centred * centred, axis=-1, keepdims=True)
-        normed[a * width : (a + 1) * width, :] = (
+        normed[a * 128 : a * 128 + width, :] = (
             centred * lax.rsqrt(variance + 1e-05) * gain + shift
         )
 
     x_rows = x_send.shape[1]
     for a in range(rows):
         for c in range(cols):
-            start = pl.multiple_of(a * width + c * devices + g * n, 8)
+            start = pl.multiple_of(a * 128 + c * devices + g * n, 8)
             stage[pl.ds(a * cols + c, n, x_rows), :] = normed[pl.ds(start, n), :]
     x_send[...] = stage[...].reshape(n, x_rows, -1).astype(BF16)
 
     w_loads[0].wait()
     b_pad[0:own_heads, :] = bias_ref[...]
     w_bias = b_pad[...]
+    part = nt_dot(w_bias, normed[...].astype(BF16))
     for a in range(rows):
-        part = nt_dot(w_bias, normed[a * width : (a + 1) * width, :].astype(BF16))
         for h in range(own_heads):
             row = h * rows + a
-            b_recv[d, g, row : row + 1, 0:width] = part[h : h + 1]
+            b_recv[d, g, row : row + 1, :] = part[h : h + 1, a * 128 : (a + 1) * 128]
+    for c in range(cols):
+        tokens[c * 128 + width : (c + 1) * 128, :] = jnp.zeros((128 - width, 128), F32)
     for copy in w_loads[1:]:
         copy.wait()
 
@@ -145,7 +147,8 @@
     def drain(ref, sem):
         pltpu.make_async_copy(ref, ref, sem).wait()
 
-    own_bias = b_recv.at[d, g]
+    b_used = own_heads * rows
+    own_bias = b_recv.at[d, g, pl.ds(0, b_used)]
     first = [(back, plane) for plane in range(groups) for back in range(slabs)][1:]
     across = {}
     for back, plane in first:
@@ -167,7 +170,7 @@
             if back or plane:
                 across[back, plane].wait_recv()
         block = slab_at[(slabs - back) % slabs] + r
-        both = b_recv.at[block]
+        both = b_recv.at[block, :, pl.ds(0, b_used)]
         for near in range(1, quad):
             send(both, both, b_send_sem.at[1], b_recv_sem.at[0], slab_at[0] + near_at[near])
 
@@ -175,7 +178,7 @@
     stage[...] = x_recv[...].reshape(n * x_rows, -1).astype(F32)
     for a in range(rows):
         for c in range(cols):
-            tokens[pl.ds(c * width + a, n, rows), :] = stage[pl.ds(a * cols + c, n, x_rows), :]
+            tokens[pl.ds(c * 128 + a, n, rows), :] = stage[pl.ds(a * cols + c, n, x_rows), :]
     entries = tokens[...].astype(BF16)
 
     w_copy.wait_recv()
@@ -184,23 +187,32 @@
         low = t * inner
         return jnp.concatenate([w_all[k, low : low + inner, :] for k in range(groups)], axis=0)
 
-    queries = nt_dot(entries, weight(0)).astype(BF16)
     keys = nt_dot(entries, weight(1)).astype(BF16)
-    w_value, w_gate = weight(2), weight(3)
-    lane = lax.broadcasted_iota(jnp.int32, (width, heads * size), 1) // size
-    scores, values, gating = [], [], []
+    channels = heads * size
+    w_rest = jnp.concatenate([weight(0), weight(2), weight(3)], axis=0)
+    rest = nt_dot(w_rest, entries)
+    queries = rest[:channels].astype(BF16)
+    all_values = rest[channels : 2 * channels].astype(BF16)
+    gating = jax.nn.sigmoid(rest[2 * channels :]).astype(BF16).astype(F32)
+    lane = lax.broadcasted_iota(jnp.int32, (width, channels), 1) // size
+    row = lax.broadcasted_iota(jnp.int32, (channels, 128), 0) // size
+    scores, values = [], []
     for c in range(cols):
-        part = slice(c * width, (c + 1) * width)
-        key = keys[part]
+        key = keys[c * 128 : c * 128 + width]
         stacked = jnp.concatenate(
             [jnp.where(lane == h, key, jnp.zeros_like(key)) for h in range(heads)], axis=0
         )
-        scores.append(nt_dot(stacked, queries[part]))
-        values.append(nt_dot(w_value, entries[part]).astype(BF16))
-        gating.append(jax.nn.sigmoid(nt_dot(w_gate, entries[part])).astype(BF16).astype(F32))
+        part = slice(c * 128, (c + 1) * 128)
+        scores.append(jnp.dot(stacked, queries[:, part], preferred_element_type=F32))
+        value = all_values[:, part]
+        values.append(
+            jnp.concatenate(
+                [jnp.where(row == h, value, jnp.zeros_like(value)) for h in range(heads)], axis=1
+            )
+        )
 
     passed = slabs * (quad - 1)
-    drain(b_recv.at[pl.ds(0, passed)], b_recv_sem.at[0])
+    drain(b_recv.at[pl.ds(0, passed), :, pl.ds(0, b_used)], b_recv_sem.at[0])
     b_rows = b_recv.shape[2]
     gathered = b_recv.reshape(n * groups * b_rows, 128)
     for h in range(heads):
@@ -211,23 +223,25 @@
             ]
 
     scale = 1.0 / math.sqrt(size)
+    blank = jnp.zeros((128 - width, 128), BF16)
     for c in range(cols):
-        parts = []
+        weights, inverse = [], []
         for h in range(heads):
             part = slice(h * width, (h + 1) * width)
-            score = scores[c][part] * scale + bias[part, 0:width]
+            score = scores[c][part] * scale + bias[part, :]
             exponent = jnp.exp(score - jnp.max(score, axis=0, keepdims=True))
             total = jnp.sum(exponent, axis=0, keepdims=True)
-            head = slice(h * size, (h + 1) * size)
-            attended = jnp.dot(values[c][head], exponent.astype(BF16), preferred_element_type=F32)
-            parts.append(attended / total * gating[c][head])
-        gated[c * width : (c + 1) * width, :] = jnp.concatenate(parts, axis=0).T
+            weights += [exponent.astype(BF16), blank]
+            inverse.append(jnp.broadcast_to(1.0 / total, (size, 128)))
+        attended = jnp.dot(values[c], jnp.concatenate(weights, axis=0), preferred_element_type=F32)
+        result = attended * jnp.concatenate(inverse, axis=0) * gating[:, c * 128 : (c + 1) * 128]
+        gated[c * 128 : (c + 1) * 128, :] = result.T
 
     g_rows = g_send.shape[1]
     for i in range(own_rows):
         for c in range(cols):
             g_stage[pl.ds(i * cols + c, devices, g_rows), :] = gated[
-                pl.ds(c * width + i, devices, own_rows), :
+                pl.ds(c * 128 + i, devices, own_rows), :
             ]
     g_send[...] = g_stage[...].reshape(devices, g_rows, -1).astype(BF16)
 
@@ -242,8 +256,8 @@
             other_g,
         )
     g_recv[me] = g_send[d * groups + g]
-    drain(b_recv.at[pl.ds(0, len(first)), 0], b_send_sem.at[0])
-    drain(b_recv.at[pl.ds(0, passed)], b_send_sem.at[1])
+    drain(b_recv.at[pl.ds(0, len(first)), 0, pl.ds(0, b_used)], b_send_sem.at[0])
+    drain(b_recv.at[pl.ds(0, passed), :, pl.ds(0, b_used)], b_send_sem.at[1])
     drain(x_send.at[pl.ds(0, n - 1)], x_send_sem)
     w_copy.wait_send()
     drain(g_send.at[pl.ds(0, devices - 1)], g_send_sem)
@@ -286,16 +300,16 @@
             pltpu.VMEM((1, channels), F32),
             pltpu.VMEM((1, channels), F32),
             pltpu.VMEM((own_heads, channels), BF16),
-            pltpu.VMEM((rows * width, channels), F32),
+            pltpu.VMEM((rows * 128, channels), F32),
             pltpu.VMEM((n * x_rows, channels), F32),
             pltpu.VMEM((n, x_rows, channels), BF16),
             pltpu.VMEM((n, x_rows, channels), BF16),
-            pltpu.VMEM((cols * width, channels), F32),
+            pltpu.VMEM((cols * 128, channels), F32),
             pltpu.VMEM((groups, w_rows, channels), BF16),
             pltpu.VMEM((16, channels), BF16),
             pltpu.VMEM((n, groups, b_rows, 128), F32),
             pltpu.VMEM((heads * width, 128), F32),
-            pltpu.VMEM((cols * width, heads * size), F32),
+            pltpu.VMEM((cols * 128, heads * size), F32),
             pltpu.VMEM((devices * g_rows, heads * size), F32),
             pltpu.VMEM((devices, g_rows, heads * size), BF16),
             pltpu.VMEM((devices, g_rows, heads * size), BF16),
@@ -392,7 +406,7 @@
     return update.astype(jnp.bfloat16)
 
 
-def fits(mesh, pair, w_bias):
+def fits(mesh, pair, w_project, w_bias):
     n, groups = mesh.shape["dap"], mesh.shape["heads"]
     rows, width, channels = pair.shape
     devices = n * groups
@@ -403,6 +417,7 @@
         and width <= 128
         and width % devices == 0
         and width % 32 == 0
+        and w_project.shape[2] * groups == 128
         and n % 8 == 0
         and rows % groups == 0
     )
@@ -412,7 +427,7 @@
     n, groups = mesh.shape["dap"], mesh.shape["heads"]
 
     def run(pair, ln_gain, ln_shift, w_project, w_bias, w_out):
-        if fits(mesh, pair, w_bias):
+        if fits(mesh, pair, w_project, w_bias):
             return fused(n, groups, pair, ln_gain, ln_shift, w_project, w_bias, w_out)
         return local(pair, ln_gain, ln_shift, w_project, w_bias, w_out)
 

time: 22.3 us -> 22 us (0.987)
  Pallas kernels: 21.5 us -> 21.2 us
    pallas_call x1, Pallas kernels: 21.5 us -> 21.2 us  [fused(): pl.pallas_call(functools.partial(kernel, dims), out_shape=pltpu.VMEM((own...]
where the time goes in v5:
time: 22 us; the launch traced here: 21.9 us
  Pallas kernels  21.2 us (96%)
  local copies, waits for them, and re-layouts  0.64 us (3%)
    pallas_call x1, Pallas kernels, fused(): pl.pallas_call(functools.partial(kernel, dims), out_shape=pltpu.VMEM((own...  21.2 us
    unnamed x1, local copies, waits for them, and re-layouts  0.64 us

profile of v5, /device:TPU:0, one launch (start us, length us, event | category | flops | bytes accessed | tf_op | source)
XLA Modules:
  0.0 21.9 jit_solution(7437872837457553596)
XLA Ops:
  0.0 21.2 %shard_map.64 = bf16[3,96,128]{2,1,0:T(8,128)(2,1)S(1)} custom-call(bf16[6,96,128]{2,1,0:T(8,128)(2,1)} %pair_hbm.1, f32[1,128]{1,0:T(1,128)} %bitcast.7, f32[1,128]{1,0:T(1,128)} %bitcast.8, bf16[2,128]{1,0:T(2,128)(2,1)} %bitcast.9, bf16[256,128]{1,0:T(8,128)(2,1)} %bitcast.6, bf16[64,128]{1,0:T(8,128)(2,1)} %w_out_hbm.1), custom_call_target="tpu_custom_call" | custom-call | tf_op jit(solution)/shard_map/pallas_call | solution.py:293
  21.2 0.6 %copy.8 = bf16[3,96,128]{2,1,0:T(8,128)(2,1)} copy(bf16[3,96,128]{2,1,0:T(8,128)(2,1)S(1)} %shard_map.64) | data formatting | bytes 147456

commit v6 on v5

--- a/solution.py
+++ b/solution.py
@@ -68,7 +68,7 @@
     d = lax.axis_index("dap")
     g = lax.axis_index("heads")
     me = g * n + d
-    quad = min(4, n)
+    quad = 4
     slabs = n // quad
     z, r = d // quad, lax.rem(d, quad)
     planes = [g, 1 - g]
@@ -124,7 +124,7 @@
     for a in range(rows):
         for h in range(own_heads):
             row = h * rows + a
-            b_recv[d, g, row : row + 1, :] = part[h : h + 1, a * 128 : (a + 1) * 128]
+            b_recv[z, r, g, row : row + 1, :] = part[h : h + 1, a * 128 : (a + 1) * 128]
     for c in range(cols):
         tokens[c * 128 + width : (c + 1) * 128, :] = jnp.zeros((128 - width, 128), F32)
     for copy in w_loads[1:]:
@@ -148,13 +148,13 @@
         pltpu.make_async_copy(ref, ref, sem).wait()
 
     b_used = own_heads * rows
-    own_bias = b_recv.at[d, g, pl.ds(0, b_used)]
+    own_bias = b_recv.at[z, r, g, pl.ds(0, b_used)]
     first = [(back, plane) for plane in range(groups) for back in range(slabs)][1:]
     across = {}
     for back, plane in first:
         k = back * groups + plane
         across[back, plane] = send(
-            own_bias, own_bias, b_send_sem.at[0], b_recv_sem.at[k], slab_at[back] + r, planes[plane]
+            own_bias, own_bias, b_send_sem.at[k], b_recv_sem.at[k], slab_at[back] + r, planes[plane]
         )
 
     far = [near + back * quad for back in range(1, slabs) for near in range(quad)]
@@ -165,14 +165,17 @@
     w_copy = send(own_w, own_w, w_send_sem, w_recv_sem, d, planes[1])
     x_recv[d] = x_send[d]
 
-    for back in range(slabs):
-        for plane in range(groups):
-            if back or plane:
-                across[back, plane].wait_recv()
-        block = slab_at[(slabs - back) % slabs] + r
-        both = b_recv.at[block, :, pl.ds(0, b_used)]
-        for near in range(1, quad):
-            send(both, both, b_send_sem.at[1], b_recv_sem.at[0], slab_at[0] + near_at[near])
+    def pass_on(place, other, k):
+        column = b_recv.at[:, place, :, pl.ds(0, b_used)]
+        return send(column, column, b_send_sem.at[k], b_recv_sem.at[k], z * quad + other)
+
+    for copy in across.values():
+        copy.wait_recv()
+    r_y = lax.rem(r + 2, quad)
+    r_core = r + 1 - 2 * lax.rem(r, 2)
+    hop = slabs * groups
+    y_copy = pass_on(r, r_y, hop)
+    core_copies = [pass_on(r, r_core, hop + 1)]
 
     drain(x_recv.at[pl.ds(0, n - 1)], x_recv_sem)
     stage[...] = x_recv[...].reshape(n * x_rows, -1).astype(F32)
@@ -211,9 +214,11 @@
             )
         )
 
-    passed = slabs * (quad - 1)
-    drain(b_recv.at[pl.ds(0, passed), :, pl.ds(0, b_used)], b_recv_sem.at[0])
-    b_rows = b_recv.shape[2]
+    y_copy.wait_recv()
+    core_copies.append(pass_on(r_y, r_core, hop + 2))
+    for copy in core_copies:
+        copy.wait_recv()
+    b_rows = b_recv.shape[3]
     gathered = b_recv.reshape(n * groups * b_rows, 128)
     for h in range(heads):
         for a in range(rows):
@@ -256,8 +261,8 @@
             other_g,
         )
     g_recv[me] = g_send[d * groups + g]
-    drain(b_recv.at[pl.ds(0, len(first)), 0, pl.ds(0, b_used)], b_send_sem.at[0])
-    drain(b_recv.at[pl.ds(0, passed), :, pl.ds(0, b_used)], b_send_sem.at[1])
+    for copy in [*across.values(), y_copy, *core_copies]:
+        copy.wait_send()
     drain(x_send.at[pl.ds(0, n - 1)], x_send_sem)
     w_copy.wait_send()
     drain(g_send.at[pl.ds(0, devices - 1)], g_send_sem)
@@ -307,7 +312,7 @@
             pltpu.VMEM((cols * 128, channels), F32),
             pltpu.VMEM((groups, w_rows, channels), BF16),
             pltpu.VMEM((16, channels), BF16),
-            pltpu.VMEM((n, groups, b_rows, 128), F32),
+            pltpu.VMEM((n // 4, 4, groups, b_rows, 128), F32),
             pltpu.VMEM((heads * width, 128), F32),
             pltpu.VMEM((cols * 128, heads * size), F32),
             pltpu.VMEM((devices * g_rows, heads * size), F32),
@@ -319,8 +324,8 @@
             sems(()),
             sems(()),
             sems(()),
-            sems((2,)),
-            sems((n // min(4, n) * groups,)),
+            sems((n // 4 * groups + 3,)),
+            sems((n // 4 * groups + 3,)),
             sems(()),
             sems(()),
         ],

time: 22 us -> 23.1 us (1.050)
  Pallas kernels: 21.2 us -> 22.3 us
    pallas_call x1, Pallas kernels: 21.2 us -> 22.3 us  [fused(): pl.pallas_call(functools.partial(kernel, dims), out_shape=pltpu.VMEM((own...]
where the time goes in v6:
time: 23.1 us; the launch traced here: 22.9 us
  Pallas kernels  22.3 us (97%)
  local copies, waits for them, and re-layouts  0.64 us (3%)
    pallas_call x1, Pallas kernels, fused(): pl.pallas_call(functools.partial(kernel, dims), out_shape=pltpu.VMEM((own...  22.3 us
    unnamed x1, local copies, waits for them, and re-layouts  0.64 us

profile of v6, /device:TPU:0, one launch (start us, length us, event | category | flops | bytes accessed | tf_op | source)
XLA Modules:
  0.0 22.9 jit_solution(537211194120057143)
XLA Ops:
  0.0 22.3 %shard_map.64 = bf16[3,96,128]{2,1,0:T(8,128)(2,1)S(1)} custom-call(bf16[6,96,128]{2,1,0:T(8,128)(2,1)} %pair_hbm.1, f32[1,128]{1,0:T(1,128)} %bitcast.7, f32[1,128]{1,0:T(1,128)} %bitcast.8, bf16[2,128]{1,0:T(2,128)(2,1)} %bitcast.9, bf16[256,128]{1,0:T(8,128)(2,1)} %bitcast.6, bf16[64,128]{1,0:T(8,128)(2,1)} %w_out_hbm.1), custom_call_target="tpu_custom_call" | custom-call | tf_op jit(solution)/shard_map/pallas_call | solution.py:298
  22.3 0.6 %copy.8 = bf16[3,96,128]{2,1,0:T(8,128)(2,1)} copy(bf16[3,96,128]{2,1,0:T(8,128)(2,1)S(1)} %shard_map.64) | data formatting | bytes 147456

commit v7 on v5

--- a/solution.py
+++ b/solution.py
@@ -110,13 +110,6 @@
             centred * lax.rsqrt(variance + 1e-05) * gain + shift
         )
 
-    x_rows = x_send.shape[1]
-    for a in range(rows):
-        for c in range(cols):
-            start = pl.multiple_of(a * 128 + c * devices + g * n, 8)
-            stage[pl.ds(a * cols + c, n, x_rows), :] = normed[pl.ds(start, n), :]
-    x_send[...] = stage[...].reshape(n, x_rows, -1).astype(BF16)
-
     w_loads[0].wait()
     b_pad[0:own_heads, :] = bias_ref[...]
     w_bias = b_pad[...]
@@ -125,11 +118,6 @@
         for h in range(own_heads):
             row = h * rows + a
             b_recv[d, g, row : row + 1, :] = part[h : h + 1, a * 128 : (a + 1) * 128]
-    for c in range(cols):
-        tokens[c * 128 + width : (c + 1) * 128, :] = jnp.zeros((128 - width, 128), F32)
-    for copy in w_loads[1:]:
-        copy.wait()
-
     pl.semaphore_wait(barrier, devices - 1)
 
     def send(src, dst, send_sem, recv_sem, other, plane=g):
@@ -157,13 +145,25 @@
             own_bias, own_bias, b_send_sem.at[0], b_recv_sem.at[k], slab_at[back] + r, planes[plane]
         )
 
+    x_rows = x_send.shape[1]
+    for a in range(rows):
+        for c in range(cols):
+            start = pl.multiple_of(a * 128 + c * devices + g * n, 8)
+            stage[pl.ds(a * cols + c, n, x_rows), :] = normed[pl.ds(start, n), :]
+    x_send[...] = stage[...].reshape(n, x_rows, -1).astype(BF16)
+
     far = [near + back * quad for back in range(1, slabs) for near in range(quad)]
     for offset in far + list(range(1, quad)):
         other = slab_at[offset // quad] + near_at[offset % quad]
         send(x_send.at[other], x_recv.at[d], x_send_sem, x_recv_sem, other)
+    for copy in w_loads[1:]:
+        copy.wait()
     own_w = w_all.at[g]
     w_copy = send(own_w, own_w, w_send_sem, w_recv_sem, d, planes[1])
     x_recv[d] = x_send[d]
+
+    for c in range(cols):
+        tokens[c * 128 + width : (c + 1) * 128, :] = jnp.zeros((128 - width, 128), F32)
 
     for back in range(slabs):
         for plane in range(groups):

time: 22 us -> 22 us (level)
  no operation moved by 1% of the time
where the time goes in v7:
time: 22 us; the launch traced here: 21.9 us
  Pallas kernels  21.2 us (96%)
  local copies, waits for them, and re-layouts  0.64 us (3%)
    pallas_call x1, Pallas kernels, fused(): pl.pallas_call(functools.partial(kernel, dims), out_shape=pltpu.VMEM((own...  21.2 us
    unnamed x1, local copies, waits for them, and re-layouts  0.64 us

profile of v7, /device:TPU:0, one launch (start us, length us, event | category | flops | bytes accessed | tf_op | source)
XLA Modules:
  0.0 21.9 jit_solution(18371652875449833240)
XLA Ops:
  0.0 21.2 %shard_map.64 = bf16[3,96,128]{2,1,0:T(8,128)(2,1)S(1)} custom-call(bf16[6,96,128]{2,1,0:T(8,128)(2,1)} %pair_hbm.1, f32[1,128]{1,0:T(1,128)} %bitcast.7, f32[1,128]{1,0:T(1,128)} %bitcast.8, bf16[2,128]{1,0:T(2,128)(2,1)} %bitcast.9, bf16[256,128]{1,0:T(8,128)(2,1)} %bitcast.6, bf16[64,128]{1,0:T(8,128)(2,1)} %w_out_hbm.1), custom_call_target="tpu_custom_call" | custom-call | tf_op jit(solution)/shard_map/pallas_call | solution.py:293
  21.2 0.6 %copy.8 = bf16[3,96,128]{2,1,0:T(8,128)(2,1)} copy(bf16[3,96,128]{2,1,0:T(8,128)(2,1)S(1)} %shard_map.64) | data formatting | bytes 147456

commit v8 on v7

--- a/solution.py
+++ b/solution.py
@@ -145,12 +145,13 @@
             own_bias, own_bias, b_send_sem.at[0], b_recv_sem.at[k], slab_at[back] + r, planes[plane]
         )
 
-    x_rows = x_send.shape[1]
+    x_used = x_send.shape[1]
+    x_rows = up(x_used, 8)
     for a in range(rows):
         for c in range(cols):
             start = pl.multiple_of(a * 128 + c * devices + g * n, 8)
             stage[pl.ds(a * cols + c, n, x_rows), :] = normed[pl.ds(start, n), :]
-    x_send[...] = stage[...].reshape(n, x_rows, -1).astype(BF16)
+    x_send[...] = stage[...].reshape(n, x_rows, -1)[:, :x_used].astype(BF16)
 
     far = [near + back * quad for back in range(1, slabs) for near in range(quad)]
     for offset in far + list(range(1, quad)):
@@ -175,7 +176,8 @@
             send(both, both, b_send_sem.at[1], b_recv_sem.at[0], slab_at[0] + near_at[near])
 
     drain(x_recv.at[pl.ds(0, n - 1)], x_recv_sem)
-    stage[...] = x_recv[...].reshape(n * x_rows, -1).astype(F32)
+    for k in range(n):
+        stage[k * x_rows : k * x_rows + x_used, :] = x_recv[k].astype(F32)
     for a in range(rows):
         for c in range(cols):
             tokens[pl.ds(c * 128 + a, n, rows), :] = stage[pl.ds(a * cols + c, n, x_rows), :]
@@ -284,7 +286,8 @@
     inner = own_heads * size
     w_rows = 5 * inner
     b_rows = up(own_heads * rows, 8)
-    x_rows = up(rows * cols, 16)
+    x_used = up(rows * cols, 2)
+    x_rows = up(x_used, 8)
     g_rows = up(own_rows * cols, 16)
     dims = (n, groups, rows, width, cols, heads, size)
     vmem = pl.BlockSpec(memory_space=pltpu.VMEM)
@@ -302,8 +305,8 @@
             pltpu.VMEM((own_heads, channels), BF16),
             pltpu.VMEM((rows * 128, channels), F32),
             pltpu.VMEM((n * x_rows, channels), F32),
-            pltpu.VMEM((n, x_rows, channels), BF16),
-            pltpu.VMEM((n, x_rows, channels), BF16),
+            pltpu.VMEM((n, x_used, channels), BF16),
+            pltpu.VMEM((n, x_used, channels), BF16),
             pltpu.VMEM((cols * 128, channels), F32),
             pltpu.VMEM((groups, w_rows, channels), BF16),
             pltpu.VMEM((16, channels), BF16),

time: 22 us -> 22 us (level)
  no operation moved by 1% of the time
where the time goes in v8:
time: 22 us; the launch traced here: 21.9 us
  Pallas kernels  21.2 us (96%)
  local copies, waits for them, and re-layouts  0.64 us (3%)
    pallas_call x1, Pallas kernels, fused(): pl.pallas_call(functools.partial(kernel, dims), out_shape=pltpu.VMEM((own...  21.2 us
    unnamed x1, local copies, waits for them, and re-layouts  0.64 us

profile of v8, /device:TPU:0, one launch (start us, length us, event | category | flops | bytes accessed | tf_op | source)
XLA Modules:
  0.0 21.9 jit_solution(15126698798762594478)
XLA Ops:
  0.0 21.2 %shard_map.64 = bf16[3,96,128]{2,1,0:T(8,128)(2,1)S(1)} custom-call(bf16[6,96,128]{2,1,0:T(8,128)(2,1)} %pair_hbm.1, f32[1,128]{1,0:T(1,128)} %bitcast.7, f32[1,128]{1,0:T(1,128)} %bitcast.8, bf16[2,128]{1,0:T(2,128)(2,1)} %bitcast.9, bf16[256,128]{1,0:T(8,128)(2,1)} %bitcast.6, bf16[64,128]{1,0:T(8,128)(2,1)} %w_out_hbm.1), custom_call_target="tpu_custom_call" | custom-call | tf_op jit(solution)/shard_map/pallas_call | solution.py:296
  21.2 0.6 %copy.8 = bf16[3,96,128]{2,1,0:T(8,128)(2,1)} copy(bf16[3,96,128]{2,1,0:T(8,128)(2,1)S(1)} %shard_map.64) | data formatting | bytes 147456

commit v9 on v5

--- a/solution.py
+++ b/solution.py
@@ -147,6 +147,11 @@
     def drain(ref, sem):
         pltpu.make_async_copy(ref, ref, sem).wait()
 
+    far = [near + back * quad for back in range(1, slabs) for near in range(quad)]
+    for offset in far + list(range(1, quad)):
+        other = slab_at[offset // quad] + near_at[offset % quad]
+        send(x_send.at[other], x_recv.at[d], x_send_sem, x_recv_sem, other)
+
     b_used = own_heads * rows
     own_bias = b_recv.at[d, g, pl.ds(0, b_used)]
     first = [(back, plane) for plane in range(groups) for back in range(slabs)][1:]
@@ -157,10 +162,6 @@
             own_bias, own_bias, b_send_sem.at[0], b_recv_sem.at[k], slab_at[back] + r, planes[plane]
         )
 
-    far = [near + back * quad for back in range(1, slabs) for near in range(quad)]
-    for offset in far + list(range(1, quad)):
-        other = slab_at[offset // quad] + near_at[offset % quad]
-        send(x_send.at[other], x_recv.at[d], x_send_sem, x_recv_sem, other)
     own_w = w_all.at[g]
     w_copy = send(own_w, own_w, w_send_sem, w_recv_sem, d, planes[1])
     x_recv[d] = x_send[d]

time: 22 us -> 24 us (1.091)
  Pallas kernels: 21.2 us -> 23.2 us
    pallas_call x1, Pallas kernels: 21.2 us -> 23.2 us  [fused(): pl.pallas_call(functools.partial(kernel, dims), out_shape=pltpu.VMEM((own...]
where the time goes in v9:
time: 24 us; the launch traced here: 23.9 us
  Pallas kernels  23.2 us (97%)
  local copies, waits for them, and re-layouts  0.64 us (3%)
    pallas_call x1, Pallas kernels, fused(): pl.pallas_call(functools.partial(kernel, dims), out_shape=pltpu.VMEM((own...  23.2 us
    unnamed x1, local copies, waits for them, and re-layouts  0.64 us

profile of v9, /device:TPU:0, one launch (start us, length us, event | category | flops | bytes accessed | tf_op | source)
XLA Modules:
  0.0 23.9 jit_solution(12641141310001374671)
XLA Ops:
  0.0 23.2 %shard_map.64 = bf16[3,96,128]{2,1,0:T(8,128)(2,1)S(1)} custom-call(bf16[6,96,128]{2,1,0:T(8,128)(2,1)} %pair_hbm.1, f32[1,128]{1,0:T(1,128)} %bitcast.7, f32[1,128]{1,0:T(1,128)} %bitcast.8, bf16[2,128]{1,0:T(2,128)(2,1)} %bitcast.9, bf16[256,128]{1,0:T(8,128)(2,1)} %bitcast.6, bf16[64,128]{1,0:T(8,128)(2,1)} %w_out_hbm.1), custom_call_target="tpu_custom_call" | custom-call | tf_op jit(solution)/shard_map/pallas_call | solution.py:294
  23.2 0.6 %copy.8 = bf16[3,96,128]{2,1,0:T(8,128)(2,1)} copy(bf16[3,96,128]{2,1,0:T(8,128)(2,1)S(1)} %shard_map.64) | data formatting | bytes 147456
